TPU v7x, 32 devices: a whole 2x2x4 slice. The times are simulated.
32 devices in a mesh: pairs: 2 (over y), pb: 4 (over z), ka: 2 (over core), wa: 2 (over x).
Axes of the slice: x: 2, y: 2, z: 4, core: 2. Of those that a mesh axis runs over, the one named last changes fastest.
Arguments:
- clean_rows: bfloat16 [4096, 8192], P(('pairs', 'pb', 'ka'), 'wa'), parts along dimension 0, may hold values from -72 to 72
- noised_rows: bfloat16 [4096, 8192], P(('pairs', 'pb', 'ka'), 'wa'), parts along dimension 0, may hold values from -6 to 6
- query_weight: bfloat16 [8192, 512], P('wa'), may hold values from -0.0625 to 0.0625
- key_weight: bfloat16 [8192, 128], P('wa'), may hold values from -0.0625 to 0.0625
- value_weight: bfloat16 [8192, 128], P('wa'), may hold values from -0.0625 to 0.0625
- out_grads: bfloat16 [4096, 512], P(('pairs', 'pb', 'ka'), 'wa'), parts along dimension 0, may hold values from -6 to 6
- lookback: int32 [4096], P('pairs'), parts along dimension 0, may hold values from 1 to 2048
Outputs:
- attribution: float32 [4096], P(('pairs', 'pb', 'ka', 'wa')), parts along dimension 0
There are 2 independent parts, one for each index of `pairs`. A program takes and returns all parts, laid end to end along the dimension named above; an argument that names none is the same for every part. Nothing has to cross between parts.
All inputs are finite; a program needn't handle non-finite values.
Results may differ from a plain program's by a relative error of at most 0.01315.
The roundings to bfloat16 on the way count: a program that leaves them out, or rounds other values in their place, can miss the bound.
Values may be sent and summed in bfloat16 or wider, within the bound.
A program may use at most 64 MiB of HBM per device.

v0:
```python
import math

import jax
import jax.numpy as jnp
from jax import lax
from jax.sharding import PartitionSpec as P

very_low = -1e30


def joined(array, axis, combine):
    everything = jax.tree.map(lambda part: lax.all_gather(part, axis), array)
    first = jax.tree.map(lambda part: part[0], everything)

    def turn(k, so_far):
        return combine(so_far, jax.tree.map(lambda part: part[k], everything))

    return lax.fori_loop(1, lax.axis_size(axis), turn, first)


def split_heads(pair_block, head_size):
    return pair_block.reshape(pair_block.shape[0], pair_block.shape[1] // head_size, head_size)


def visible_pairs(query_pos, query_look, key_pos):
    distance = query_pos[:, None] - key_pos[None, :]
    return (distance >= 0) & (distance < query_look[:, None])


def combine_stats(earlier, later):
    highest = jnp.maximum(earlier[0], later[0])
    left_scale = jnp.exp(earlier[0] - highest)
    right_scale = jnp.exp(later[0] - highest)
    return (
        highest,
        earlier[1] * left_scale + later[1] * right_scale,
        earlier[2] * left_scale + later[2] * right_scale,
    )


def block_stats(
    query_block, grad_block, query_pos, query_look, key_block, value_block, key_pos, score_scale
):
    scores = (
        jnp.einsum("bhd,kd->bhk", query_block, key_block, preferred_element_type=jnp.float32)
        * score_scale
    )
    grad_value = jnp.einsum(
        "bhd,kd->bhk", grad_block, value_block, preferred_element_type=jnp.float32
    )
    visible = visible_pairs(query_pos, query_look, key_pos)[:, None, :]
    masked = jnp.where(visible, scores, very_low)
    highest = jnp.max(masked, axis=2)
    weights = jnp.where(visible, jnp.exp(masked - highest[:, :, None]), 0.0)
    return (highest, jnp.sum(weights, axis=2), jnp.sum(weights * grad_value, axis=2))


def block_changes(
    query_block,
    grad_block,
    query_pos,
    query_look,
    row_parts,
    key_block,
    value_block,
    noised_block,
    key_pos,
    score_scale,
):
    highest, row_total, weighted, mean_now = row_parts
    scores = (
        jnp.einsum("bhd,kd->bhk", query_block, key_block, preferred_element_type=jnp.float32)
        * score_scale
    )
    patched = (
        jnp.einsum("bhd,kd->bhk", query_block, noised_block, preferred_element_type=jnp.float32)
        * score_scale
    )
    grad_value = jnp.einsum(
        "bhd,kd->bhk", grad_block, value_block, preferred_element_type=jnp.float32
    )
    visible = visible_pairs(query_pos, query_look, key_pos)[:, None, :]
    held = highest[:, :, None]
    scores = jnp.where(visible, scores, held)
    patched = jnp.where(visible, patched, held)
    shifted = jnp.maximum(held, patched)
    factor = jnp.exp(held - shifted)
    swapped = jnp.exp(patched - shifted) - jnp.exp(scores - shifted)
    divisor = jnp.maximum(row_total[:, :, None] * factor + swapped, 1.0)
    change = (weighted[:, :, None] * factor + swapped * grad_value) / divisor - mean_now[:, :, None]
    return jnp.sum(jnp.where(visible, change, 0.0), axis=(0, 1))


def tile_stats(pair_piece, query_pos, query_look, key_tile, key_pos, score_scale, head_size):
    row_count = pair_piece.shape[0]
    head_cols = pair_piece.shape[1] // 2
    block_rows = math.gcd(row_count, 512)
    key_count = key_tile.shape[0]
    key_width = math.gcd(key_count, 1024)

    def one_block(block_index):
        offset = block_index * block_rows
        pair_block = lax.dynamic_slice_in_dim(pair_piece, offset, block_rows, 0)
        query_block = split_heads(pair_block[:, :head_cols], head_size)
        grad_block = split_heads(pair_block[:, head_cols:], head_size)
        block_pos = lax.dynamic_slice_in_dim(query_pos, offset, block_rows, 0)
        block_look = lax.dynamic_slice_in_dim(query_look, offset, block_rows, 0)
        head_count = query_block.shape[1]

        def one_key(running, key_index):
            key_offset = key_index * key_width
            key_block = lax.dynamic_slice(key_tile, (key_offset, 0), (key_width, head_size))
            value_block = lax.dynamic_slice(
                key_tile, (key_offset, head_size), (key_width, head_size)
            )
            block_keys = lax.dynamic_slice_in_dim(key_pos, key_offset, key_width, 0)
            block_part = block_stats(
                query_block,
                grad_block,
                block_pos,
                block_look,
                key_block,
                value_block,
                block_keys,
                score_scale,
            )
            return (combine_stats(running, block_part), None)

        empty_rows = jnp.zeros((block_rows, head_count), jnp.float32)
        start_stats = (
            jnp.full((block_rows, head_count), very_low, jnp.float32),
            empty_rows,
            empty_rows,
        )
        result, _ = lax.scan(
            one_key, start_stats, jnp.arange(key_count // key_width, dtype=jnp.int32)
        )
        return result

    if block_rows == row_count:
        return one_block(0)
    stacked = lax.map(one_block, jnp.arange(row_count // block_rows, dtype=jnp.int32))
    return tuple((member.reshape(row_count, member.shape[2]) for member in stacked))


def tile_changes(
    pair_tile, query_pos, query_look, merged_stats, key_tile, key_pos, score_scale, head_size
):
    row_count = pair_tile.shape[0]
    head_cols = pair_tile.shape[1] // 2
    block_rows = math.gcd(row_count, 512)
    key_count = key_tile.shape[0]
    key_width = math.gcd(key_count, 1024)
    highest, row_total, weighted = merged_stats
    row_parts = (highest, row_total, weighted, weighted / row_total)

    def one_block(running, block_index):
        offset = block_index * block_rows
        pair_block = lax.dynamic_slice_in_dim(pair_tile, offset, block_rows, 0)
        query_block = split_heads(pair_block[:, :head_cols], head_size)
        grad_block = split_heads(pair_block[:, head_cols:], head_size)
        block_pos = lax.dynamic_slice_in_dim(query_pos, offset, block_rows, 0)
        block_look = lax.dynamic_slice_in_dim(query_look, offset, block_rows, 0)
        block_rows_stats = tuple(
            (lax.dynamic_slice_in_dim(member, offset, block_rows, 0) for member in row_parts)
        )

        def one_key(key_index):
            key_offset = key_index * key_width
            key_block = lax.dynamic_slice(key_tile, (key_offset, 0), (key_width, head_size))
            value_block = lax.dynamic_slice(
                key_tile, (key_offset, head_size), (key_width, head_size)
            )
            noised_block = lax.dynamic_slice(
                key_tile, (key_offset, 2 * head_size), (key_width, head_size)
            )
            block_keys = lax.dynamic_slice_in_dim(key_pos, key_offset, key_width, 0)
            return block_changes(
                query_block,
                grad_block,
                block_pos,
                block_look,
                block_rows_stats,
                key_block,
                value_block,
                noised_block,
                block_keys,
                score_scale,
            )

        changes = lax.map(one_key, jnp.arange(key_count // key_width, dtype=jnp.int32))
        return (running + changes.reshape(key_count), None)

    summed, _ = lax.scan(
        one_block,
        jnp.zeros((key_count,), jnp.float32),
        jnp.arange(row_count // block_rows, dtype=jnp.int32),
    )
    return summed


def shards(clean_rows, noised_rows, query_weight, key_weight, value_weight, out_grads, lookback):
    head_size = key_weight.shape[1]
    score_scale = 1.0 / math.sqrt(head_size)
    pb_size = lax.axis_size("pb")
    ka_size = lax.axis_size("ka")
    pb_index = lax.axis_index("pb")
    ka_index = lax.axis_index("ka")
    pair_rows = clean_rows.shape[0]
    side_weight = jnp.concatenate([key_weight, value_weight], axis=1)
    query_terms = jnp.dot(clean_rows, query_weight, preferred_element_type=jnp.float32)
    queries = lax.psum_scatter(query_terms, "wa", scatter_dimension=1, tiled=True).astype(
        jnp.bfloat16
    )
    key_side = lax.psum_scatter(
        jnp.concatenate(
            [
                jnp.dot(clean_rows, side_weight, preferred_element_type=jnp.float32),
                jnp.dot(noised_rows, key_weight, preferred_element_type=jnp.float32),
            ],
            axis=1,
        ),
        "wa",
        scatter_dimension=0,
        tiled=True,
    ).astype(jnp.bfloat16)
    pair_data = jnp.concatenate([queries, out_grads], axis=1)
    look_grid = lookback.reshape(pb_size, ka_size, pair_rows)
    tile_base = pb_index * (ka_size * pair_rows)
    key_tile = lax.all_gather(key_side, ("pb", "wa"), axis=0, tiled=True)
    row_ids = jnp.arange(key_tile.shape[0], dtype=jnp.int32)
    key_pos = (
        row_ids // pair_rows * (ka_size * pair_rows) + ka_index * pair_rows + row_ids % pair_rows
    )
    look_tile = lax.dynamic_index_in_dim(look_grid, pb_index, 0, keepdims=False).reshape(-1)
    pair_piece = lax.all_gather(pair_data, "ka", axis=0, tiled=True)
    row_ids = jnp.arange(pair_piece.shape[0], dtype=jnp.int32)
    highest, row_total, weighted, pair_tile = tile_stats(
        pair_piece, tile_base + row_ids, look_tile, key_tile, key_pos, score_scale, head_size
    ) + (pair_piece,)
    merged_stats = joined((highest, row_total, weighted), "ka", combine_stats)
    query_pos = tile_base + jnp.arange(pair_tile.shape[0], dtype=jnp.int32)
    key_part = tile_changes(
        pair_tile, query_pos, look_tile, merged_stats, key_tile, key_pos, score_scale, head_size
    )
    return lax.psum_scatter(key_part, ("pb", "wa"), scatter_dimension=0, tiled=True)


def solution(mesh):
    in_specs = (
        P(("pairs", "pb", "ka"), "wa"),
        P(("pairs", "pb", "ka"), "wa"),
        P("wa", None),
        P("wa", None),
        P("wa", None),
        P(("pairs", "pb", "ka"), "wa"),
        P("pairs"),
    )
    out_specs = P(("pairs", "pb", "ka", "wa"))
    return jax.shard_map(shards, mesh=mesh, in_specs=in_specs, out_specs=out_specs, check_vma=False)
```

profile of v0, /device:TPU:0, one launch (start us, length us, event | category | flops | bytes accessed | tf_op | source)
XLA Modules:
  0.0 102.5 jit_solution(1232725400893335930)
XLA Ops:
  6.5 0.0 copy-start
  6.5 0.0 reduce-scatter.5.cloned.1.call-start
  6.5 2.8 %fusion.47 = f32[256,128]{0,1:T(8,128)S(1)} fusion(bf16[256,4096]{1,0:T(8,128)(2,1)} %param.8, bf16[4096,128]{1,0:T(8,128)(2,1)} %param.10), kind=kOutput, calls=%fused_computation.77 | convolution fusion | flops 268435456 | bytes 3276800 | tf_op jit(solution)/shard_map/dot_general | solution.py:219
  9.4 0.0 copy-done
  9.4 2.3 %fusion.10 = f32[256,256]{0,1:T(8,128)S(1)} fusion(bf16[256,4096]{1,0:T(8,128)(2,1)S(1)} %copy-done, bf16[4096,128]{1,0:T(8,128)(2,1)} %param.11, bf16[4096,128]{1,0:T(8,128)(2,1)} %param.10), kind=kOutput, calls=%fused_computation.19 | convolution fusion | flops 541065216 | bytes 4456448 | tf_op jit(solution)/shard_map/dot_general | solution.py:218
  11.7 0.8 pad_maximum_fusion
  12.5 0.0 reduce-scatter.5.cloned.1.call-update
  12.5 0.0 copy-start.2
  12.5 0.0 copy-start.3
  12.5 0.0 copy-start.1
  12.5 0.0 reduce-scatter.3.cloned.1.call-start
  12.6 4.3 %fusion.46 = f32[256,512]{1,0:T(8,128)} fusion(bf16[256,4096]{1,0:T(8,128)(2,1)S(1)} %copy-done, bf16[4096,512]{1,0:T(8,128)(2,1)} %param.9), kind=kOutput, calls=%fused_computation.76 | convolution fusion | flops 1073741824 | bytes 6815744 | tf_op jit(solution)/shard_map/dot_general | solution.py:211
  16.8 0.0 reduce-scatter.3.cloned.1.call-update
  16.9 0.0 copy-done.2
  16.9 0.0 copy-done.3
  16.9 0.6 dynamic-slice
  18.2 0.6 fusion.9
  18.8 9.6 %reduce-scatter.5.cloned.1.call-done = f32[128,384]{0,1:T(8,128)} async-done(((f32[256,384]{0,1:T(8,128)}), f32[128,384]{0,1:T(8,128)}) %reduce-scatter.5.cloned.1.call-update) | async-done | bytes 196624 | tf_op jit(solution)/shard_map/reduce_scatter | solution.py:215
  28.5 0.9 convert_element_type.7
  29.4 31.6 %all_gather.19 = bf16[1024,384]{0,1:T(8,128)(2,1)S(1)} all-gather(bf16[128,384]{0,1:T(8,128)(2,1)S(1)} %convert_element_type.7), channel_id=1, replica_groups=mesh['pairs'=2,'pb'=4,'ka'=2,'wa'=2] {'pb','wa'}, dimensions={0}, use_global_device_ids=true | all-gather | bytes 884736 | tf_op jit(solution)/shard_map/all_gather | solution.py:230
  61.0 0.0 reduce-scatter.3.cloned.1.call-done
  61.0 1.0 convert_element_type.6
  62.0 0.0 copy-done.1
  62.0 2.2 %all_gather.18 = bf16[512,512]{1,0:T(8,128)(2,1)S(1)} all-gather(bf16[256,512]{1,0:T(8,128)(2,1)S(1)} %pad_maximum_fusion.1), channel_id=1, replica_groups=mesh['pairs'=2,'pb'=4,'ka'=2,'wa'=2] {'ka'}, dimensions={0}, use_global_device_ids=true | all-gather | bytes 786432 | tf_op jit(solution)/shard_map/all_gather | solution.py:236
  64.3 1.1 %select_reduce_fusion.1 = (f32[512,2]{0,1:T(2,128)S(1)}, f32[512,2,1024]{2,0,1:T(8,128)S(1)}) fusion(pred[512,1024]{1,0:T(8,128)(4,1)S(1)} %fusion.9, bf16[1024,384]{0,1:T(8,128)(2,1)S(1)} %all_gather.19, bf16[64,2,8,128]{3,2,1,0:T(8,128)(2,1)S(1)} %get-tuple-element.110), kind=kOutput, calls=%fused_computation.10 | convolution fusion | flops 271580160 | bytes 5246976 | tf_op jit(solution)/shard_map/while/body/eval_jaxpr/bhd,kd->bhk/dot_general | solution.py:45
  65.4 2.0 %fusion.4 = (f32[512,2]{0,1:T(2,128)S(1)}, f32[512,2]{0,1:T(2,128)S(1)}, f32[512,2,1024]{2,0,1:T(8,128)S(1)}) fusion(f32[512,2,1024]{2,0,1:T(8,128)S(1)} %get-tuple-element.116, f32[512,2]{0,1:T(2,128)S(1)} %get-tuple-element.115, pred[512,1024]{1,0:T(8,128)(4,1)S(1)} %fusion.9, bf16[1024,384]{0,1:T(8,128)(2,1)S(1)} %all_gather.19, ...), kind=kOutput, calls=%fused_computation.13 | convolution fusion | flops 275773440 | bytes 9449472 | tf_op jit(solution)/shard_map/while/body/eval_jaxpr/bhd,kd->bhk/dot_general | solution.py:48
  67.3 1.8 %all_gather.20 = f32[2,512,2]{1,2,0:T(2,128)S(1)} all-gather(f32[1,512,2]{1,2,0:T(2,128)S(1)} %get-tuple-element.112), channel_id=1, replica_groups=mesh['pairs'=2,'pb'=4,'ka'=2,'wa'=2] {'ka'}, dimensions={0}, use_global_device_ids=true | all-gather | bytes 12288 | tf_op jit(solution)/shard_map/all_gather | solution.py:12
  69.1 1.8 %all_gather.21 = f32[2,512,2]{1,2,0:T(2,128)S(1)} all-gather(f32[1,512,2]{1,2,0:T(2,128)S(1)} %get-tuple-element.114), channel_id=1, replica_groups=mesh['pairs'=2,'pb'=4,'ka'=2,'wa'=2] {'ka'}, dimensions={0}, use_global_device_ids=true | all-gather | bytes 12288 | tf_op jit(solution)/shard_map/all_gather | solution.py:12
  70.9 1.8 %all_gather.22 = f32[2,512,2]{1,2,0:T(2,128)S(1)} all-gather(f32[1,512,2]{1,2,0:T(2,128)S(1)} %get-tuple-element.113), channel_id=1, replica_groups=mesh['pairs'=2,'pb'=4,'ka'=2,'wa'=2] {'ka'}, dimensions={0}, use_global_device_ids=true | all-gather | bytes 12288 | tf_op jit(solution)/shard_map/all_gather | solution.py:12
  72.7 4.5 %select_reduce_fusion = f32[1024]{0:T(1024)S(1)} fusion(f32[512,2,1024]{2,0,1:T(8,128)S(1)} %get-tuple-element.117, f32[512,2,1024]{2,0,1:T(8,128)S(1)} %get-tuple-element.116, f32[512,2]{0,1:T(2,128)S(1)} %get-tuple-element.94, f32[512,2]{0,1:T(2,128)S(1)} %get-tuple-element.107, f32[512,2]{0,1:T(2,128)S(1)} %get-tuple-element.109, ...), kind=kOutput, calls=%fused_computation.7 | convolution fusion | flops 288357376 | bytes 9457664 | tf_op jit(solution)/shard_map/while/body/eval_jaxpr/while/body/eval_jaxpr/bhd,kd->bhk/dot_general | solution.py:76
  77.3 17.8 %all-reduce = f32[1024]{0:T(1024)S(1)} all-reduce(f32[1024]{0:T(1024)S(1)} %select_reduce_fusion), channel_id=4, replica_groups=mesh['pairs'=2,'pb'=4,'ka'=2,'wa'=2] {'pb','wa'}, use_global_device_ids=true, to_apply=%region_6.7.clone | all-reduce | flops 1024 | bytes 8192
  95.1 0.6 dynamic-slice.1
  (9 shorter events, 0.1 us)
Async XLA Ops:
  6.5 2.8 %copy-start = (bf16[256,4096]{1,0:T(8,128)(2,1)S(1)}, bf16[256,4096]{1,0:T(8,128)(2,1)}, u32[]{:S(2)}) copy-start(bf16[256,4096]{1,0:T(8,128)(2,1)} %param.7) | copy-start | bytes 6291460
  6.5 21.9 %reduce-scatter.5.cloned.1.call-start = ((), (), s32[]{:S(2)}) async-start(), calls=%async_computation.3 | async-start | bytes 589824 | tf_op jit(solution)/shard_map/reduce_scatter | solution.py:215
  12.5 4.4 %copy-start.2 = (s32[2048]{0:T(1024)S(1)}, s32[2048]{0:T(1024)}, u32[]{:S(2)}) copy-start(s32[2048]{0:T(1024)} %param.13) | copy-start | bytes 24580
  12.5 4.4 %copy-start.3 = (u32[32]{0:T(128)S(1)}, u32[32]{0:T(128)}, u32[]{:S(2)}) copy-start(u32[32]{0:T(128)} %constant.133) | copy-start | bytes 388
  12.5 49.5 %copy-start.1 = (bf16[256,256]{1,0:T(8,128)(2,1)S(1)}, bf16[256,256]{1,0:T(8,128)(2,1)}, u32[]{:S(2)}) copy-start(bf16[256,256]{1,0:T(8,128)(2,1)} %param.12) | copy-start | bytes 393220
  12.5 48.5 %reduce-scatter.3.cloned.1.call-start = ((), (), s32[]{:S(2)}) async-start(), calls=%async_computation.2 | async-start | bytes 786432 | tf_op jit(solution)/shard_map/reduce_scatter | solution.py:212
Sparse Core Ops, SparseCore 0:
  12.6 15.7 reduce-scatter.4
  30.8 22.7 reduce-scatter.2
where the time goes:
time: 103 us
  blocking collectives  57 us (55%)
  matrix products  17 us (17%)
  between operations  14.2 us (14%)
  waiting for transfers between devices  9.68 us (9%)
  other arithmetic  3.36 us (3%)
  local copies, waits for them, and re-layouts  1.25 us (1%)
    all_gather x1, blocking collectives, shards(): key_tile = lax.all_gather(key_side, ('pb', 'wa'), axis=0, tiled=True)  31.6 us
    unnamed x1, blocking collectives  17.8 us
    reduce_scatter x1, waiting for transfers between devices, shards(): lax.psum_scatter(jnp.concatenate([jnp.dot(clean_rows, side_weight, prefer...  9.64 us
    all_gather x3, blocking collectives, joined(): everything = jax.tree.map(lambda part: lax.all_gather(part, axis), array)  5.36 us
    dot_general x1, matrix products, block_changes(): jnp.einsum('bhd,kd->bhk', query_block, noised_block, preferred_element_ty...  4.55 us
    dot_general x1, matrix products, shards(): jnp.dot(clean_rows, query_weight, preferred_element_type=jnp.float32)  4.25 us
    dot_general x1, matrix products, shards(): jnp.dot(noised_rows, key_weight, preferred_element_type=jnp.float32)  2.82 us
    dot_general x1, matrix products, shards(): jnp.dot(clean_rows, side_weight, preferred_element_type=jnp.float32)  2.3 us
  transfers between devices with their start and end apart: 2, of which 1 were waited for; matrix products, arithmetic and copies ran while one was open for 6% of the time, Pallas kernels for 0%

commit v1 on v0

v1 whole, which is shorter than its diff:
```python
import functools
import math

import jax
import jax.numpy as jnp
from jax import lax
from jax.experimental import pallas as pl
from jax.experimental.pallas import tpu as pltpu
from jax.sharding import PartitionSpec as P

very_low = -1e30
keep_limit = 24 * 2**20
vmem_limit = 56 * 2**20
MESH = pl.DeviceIdType.MESH


def dot(left, right):
    return jnp.dot(left, right, preferred_element_type=jnp.float32)


def dot_t(left, right):
    return lax.dot_general(
        left, right, (((1,), (1,)), ((), ())), preferred_element_type=jnp.float32
    )


def kernel(
    sizes,
    clean_hbm,
    noised_hbm,
    wq_hbm,
    wk_hbm,
    wv_hbm,
    grad_hbm,
    look_ref,
    out_ref,
    clean,
    noised,
    wq,
    wkv,
    grad,
    kv_part,
    nk_part,
    q_part,
    kv_in,
    nk_in,
    q_in,
    side,
    qs,
    gs,
    kept,
    top,
    total,
    weighted,
    mean,
    lane_sum,
    att,
    att_in,
    load_sem,
    kv_send,
    kv_recv,
    nk_send,
    nk_recv,
    q_send,
    q_recv,
    ag_send,
    ag_recv,
    z_send,
    z_recv,
    sib_send,
    sib_recv,
    att_send,
    att_recv,
):
    pb, ka, wa, rows, hd, heads, keep = sizes
    piece = rows // wa
    head_cols = heads * hd
    lanes = heads * rows
    scale = math.log2(math.e) / math.sqrt(hd)
    members = pb * ka * wa
    z = lax.axis_index("pb")
    c = lax.axis_index("ka")
    x = lax.axis_index("wa")
    me = (z * ka + c) * wa + x

    def peer(o):
        return lax.rem(x + o, wa)

    loads = [
        pltpu.make_async_copy(clean_hbm, clean, load_sem.at[0]),
        pltpu.make_async_copy(wk_hbm, wkv.at[:, pl.ds(0, hd)], load_sem.at[1]),
        pltpu.make_async_copy(wv_hbm, wkv.at[:, pl.ds(hd, hd)], load_sem.at[2]),
        pltpu.make_async_copy(noised_hbm, noised, load_sem.at[3]),
    ]
    orders = list(range(1, wa)) + [0]
    for o in orders:
        cols = pl.ds(pl.multiple_of(peer(o) * head_cols, 128), head_cols)
        loads.append(pltpu.make_async_copy(wq_hbm.at[:, cols], wq.at[o], load_sem.at[5 + o]))
    loads.append(pltpu.make_async_copy(grad_hbm, grad, load_sem.at[4]))
    for load in loads:
        load.start()

    barrier = pltpu.get_barrier_semaphore()

    def place(t):
        return {"pb": t // (ka * wa), "ka": (t // wa) % ka, "wa": t % wa}

    def greet(t, carry):
        @pl.when(t != me)
        def _():
            pl.semaphore_signal(barrier, inc=1, device_id=place(t), device_id_type=MESH)

        return carry

    lax.fori_loop(0, members, greet, 0)

    def remote(src, dst, send, recv, where):
        return pltpu.make_async_remote_copy(
            src_ref=src,
            dst_ref=dst,
            send_sem=send,
            recv_sem=recv,
            device_id=where,
            device_id_type=MESH,
        )

    def part_rows(p):
        return pl.ds(pl.multiple_of(p * piece, piece), piece)

    for load in loads[:3]:
        load.wait()
    kv_part[...] = dot(clean[...], wkv[...])
    pl.semaphore_wait(barrier, members - 1)
    kv_copies = []
    for o in range(1, wa):
        p = peer(o)
        copy = remote(
            kv_part.at[part_rows(p)], kv_in.at[wa - o], kv_send.at[o], kv_recv.at[wa - o], {"wa": p}
        )
        copy.start()
        kv_copies.append(copy)
    loads[3].wait()
    nk_part[...] = dot(noised[...], wkv[:, :hd])
    nk_copies = []
    for o in range(1, wa):
        p = peer(o)
        copy = remote(
            nk_part.at[part_rows(p)], nk_in.at[wa - o], nk_send.at[o], nk_recv.at[wa - o], {"wa": p}
        )
        copy.start()
        nk_copies.append(copy)
    q_copies = []
    for n, o in enumerate(orders):
        loads[4 + n].wait()
        q_part[o] = dot(clean[...], wq[o])
        if o:
            copy = remote(
                q_part.at[o], q_in.at[wa - o], q_send.at[o], q_recv.at[wa - o], {"wa": peer(o)}
            )
            copy.start()
            q_copies.append(copy)

    mine = part_rows(x)
    for copy in kv_copies:
        copy.wait_recv()
    kv_sum = kv_part[mine, :]
    for o in range(1, wa):
        kv_sum = kv_sum + kv_in[o]
    side[z, c, mine, pl.ds(0, 2 * hd)] = kv_sum.astype(jnp.bfloat16)
    for copy in nk_copies:
        copy.wait_recv()
    nk_sum = nk_part[mine, :]
    for o in range(1, wa):
        nk_sum = nk_sum + nk_in[o]
    side[z, c, mine, pl.ds(2 * hd, hd)] = nk_sum.astype(jnp.bfloat16)
    ag_copies = []
    for o in range(1, wa):
        own = side.at[z, c, mine]
        copy = remote(own, own, ag_send.at[o], ag_recv.at[wa - o], {"wa": peer(o)})
        copy.start()
        ag_copies.append(copy)
    for o in range(1, wa):
        theirs = side.at[z, c, part_rows(peer(wa - o))]
        remote(theirs, theirs, ag_send.at[o], ag_recv.at[wa - o], {"wa": peer(o)}).wait_recv()

    def up(zz):
        block = side.at[zz, c]
        return remote(block, block, z_send.at[zz], z_recv.at[zz], {"pb": z + 1})

    def across(zz, o):
        block = side.at[zz, c]
        return remote(
            block, block, sib_send.at[zz, o], sib_recv.at[zz, ka - o], {"ka": lax.rem(c + o, ka)}
        )

    def pass_on(zz):
        @pl.when(z + 1 < pb)
        def _():
            up(zz).start()

        for o in range(1, ka):

            @pl.when((zz < z) | (c + o < ka))
            def _():
                across(zz, o).start()

    def arrive(zz):
        block = side.at[zz, c]
        remote(block, block, z_send.at[zz], z_recv.at[zz], {"pb": z - 1}).wait_recv()
        pass_on(zz)

    pass_on(z)

    @pl.when(z >= 1)
    def _():
        arrive(z - 1)

    loads[-1].wait()
    for copy in q_copies:
        copy.wait_recv()
    q_sum = q_part[0]
    for o in range(1, wa):
        q_sum = q_sum + q_in[o]
    q_sum = q_sum.astype(jnp.bfloat16)
    for h in range(heads):
        qs[pl.ds(h * rows, rows), :] = q_sum[:, h * hd : (h + 1) * hd]
        gs[pl.ds(h * rows, rows), :] = grad[:, h * hd : (h + 1) * hd]

    group_rows = rows // 128
    first_look = (z * ka + c) * group_rows
    look = jnp.concatenate(
        [look_ref[pl.ds(first_look + i, 1), :] for i in range(group_rows)] * heads, axis=1
    )
    last_key = (z * ka + c) * rows + jnp.concatenate(
        [lax.broadcasted_iota(jnp.int32, (1, rows), 1)] * heads, axis=1
    )
    before_key = last_key - look

    def products(zz, cc):
        key_pos = (zz * ka + cc) * rows + lax.broadcasted_iota(jnp.int32, (rows, lanes), 0)
        visible = (key_pos <= last_key) & (key_pos > before_key)
        scores = dot_t(side[zz, cc, :, pl.ds(0, hd)], qs[...]) * scale
        patched = dot_t(side[zz, cc, :, pl.ds(2 * hd, hd)], qs[...]) * scale
        grad_value = dot_t(side[zz, cc, :, pl.ds(hd, hd)], gs[...])
        return (
            jnp.where(visible, scores, very_low),
            jnp.where(visible, patched, very_low),
            grad_value,
        )

    top[...] = jnp.full((1, lanes), very_low, jnp.float32)
    total[...] = jnp.zeros((1, lanes), jnp.float32)
    weighted[...] = jnp.zeros((1, lanes), jnp.float32)

    def stats(zz, cc):
        scores, patched, grad_value = products(zz, cc)
        if keep:
            kept[zz, cc, 0] = scores
            kept[zz, cc, 1] = patched
            kept[zz, cc, 2] = grad_value
        highest = jnp.maximum(top[...], jnp.max(scores, axis=0, keepdims=True))
        rescale = jnp.exp2(top[...] - highest)
        weights = jnp.exp2(scores - highest)
        total[...] = total[...] * rescale + jnp.sum(weights, axis=0, keepdims=True)
        weighted[...] = weighted[...] * rescale + jnp.sum(
            weights * grad_value, axis=0, keepdims=True
        )
        top[...] = highest

    def other_stats(zz, o):
        cc = lax.rem(c + ka - o, ka)
        block = side.at[zz, cc]
        remote(block, block, sib_send.at[zz, o], sib_recv.at[zz, ka - o], {"ka": cc}).wait_recv()
        stats(zz, cc)

    stats(z, c)
    for o in range(1, ka):

        @pl.when(c >= o)
        def _():
            other_stats(z, o)

    def earlier(s, carry):
        @pl.when(s <= z)
        def _():
            @pl.when(s >= 2)
            def _():
                arrive(z - s)

            stats(z - s, c)
            for o in range(1, ka):
                other_stats(z - s, o)

        return carry

    lax.fori_loop(1, pb, earlier, 0)

    mean[...] = weighted[...] / jnp.maximum(total[...], 1.0)

    step = 64

    def att_copy(t):
        return remote(att.at[t], att_in.at[me], att_send.at[t], att_recv.at[me], place(t))

    def changes(b, carry):
        zz, cc = b // ka, b % ka

        @pl.when(b <= z * ka + c)
        def _():
            if not keep:
                scores, patched, grad_value = products(zz, cc)
                kept[0, 0, 0] = scores
                kept[0, 0, 1] = patched
                kept[0, 0, 2] = grad_value
            kz, kc = (zz, cc) if keep else (0, 0)

            def chunk(k, carry):
                keys = pl.ds(pl.multiple_of(k * step, step), step)
                so_far = jnp.zeros((step, 128), jnp.float32)
                for q in range(lanes // 128):
                    cols = pl.ds(q * 128, 128)
                    high = top[:, cols]
                    sums = weighted[:, cols]
                    away = kept[kz, kc, 1, keys, cols] - high
                    small = jnp.exp2(-jnp.abs(away))
                    above = away > 0.0
                    factor = jnp.where(above, small, 1.0)
                    swapped = (
                        jnp.where(above, 1.0, small)
                        - jnp.exp2(kept[kz, kc, 0, keys, cols] - high) * factor
                    )
                    divisor = jnp.maximum(total[:, cols] * factor + swapped, 1.0)
                    so_far = so_far + (
                        (sums * factor + swapped * kept[kz, kc, 2, keys, cols]) / divisor
                        - mean[:, cols]
                    )
                lane_sum[keys, :] = so_far
                return carry

            lax.fori_loop(0, rows // step, chunk, 0)
            row = jnp.sum(jnp.transpose(lane_sum[...]), axis=0, keepdims=True)
            for p in range(wa):
                att[b * wa + p] = row[:, p * piece : (p + 1) * piece]

                @pl.when(b * wa + p != me)
                def _():
                    att_copy(b * wa + p).start()

        return carry

    lax.fori_loop(0, pb * ka, changes, 0)

    out_ref[...] = att[me]

    def collect(t, carry):
        @pl.when((t != me) & (t // wa >= z * ka + c))
        def _():
            remote(
                att.at[t], att_in.at[t], att_send.at[t], att_recv.at[t], place(t)
            ).wait_recv()
            out_ref[...] += att_in[t]

        return carry

    lax.fori_loop(0, members, collect, 0)

    for copy in kv_copies + nk_copies + q_copies + ag_copies:
        copy.wait_send()

    def drain(zz, carry):
        @pl.when(zz <= z)
        def _():
            @pl.when(z + 1 < pb)
            def _():
                up(zz).wait_send()

            for o in range(1, ka):

                @pl.when((zz < z) | (c + o < ka))
                def _():
                    across(zz, o).wait_send()

        return carry

    lax.fori_loop(0, pb, drain, 0)

    def drain_att(t, carry):
        @pl.when((t != me) & (t // wa <= z * ka + c))
        def _():
            att_copy(t).wait_send()

        return carry

    lax.fori_loop(0, members, drain_att, 0)


def shards(clean_rows, noised_rows, query_weight, key_weight, value_weight, out_grads, lookback):
    pb, ka, wa = lax.axis_size("pb"), lax.axis_size("ka"), lax.axis_size("wa")
    rows, depth = clean_rows.shape
    hd = key_weight.shape[1]
    head_cols = out_grads.shape[1]
    heads = head_cols // hd
    lanes = heads * rows
    piece = rows // wa
    members = pb * ka * wa
    block = 3 * rows * lanes * 4
    keep = pb * ka * block <= keep_limit
    kept_shape = (pb, ka, 3, rows, lanes) if keep else (1, 1, 3, rows, lanes)
    sizes = (pb, ka, wa, rows, hd, heads, keep)
    bf16, f32 = jnp.bfloat16, jnp.float32
    vmem = pltpu.VMEM
    sem = pltpu.SemaphoreType.DMA
    out = pl.pallas_call(
        functools.partial(kernel, sizes),
        out_shape=jax.ShapeDtypeStruct((1, piece), f32),
        in_specs=[pl.BlockSpec(memory_space=pl.ANY)] * 6 + [pl.BlockSpec(memory_space=vmem)],
        out_specs=pl.BlockSpec(memory_space=vmem),
        scratch_shapes=[
            vmem((rows, depth), bf16),
            vmem((rows, depth), bf16),
            vmem((wa, depth, head_cols), bf16),
            vmem((depth, 2 * hd), bf16),
            vmem((rows, head_cols), bf16),
            vmem((rows, 2 * hd), f32),
            vmem((rows, hd), f32),
            vmem((wa, rows, head_cols), f32),
            vmem((wa, piece, 2 * hd), f32),
            vmem((wa, piece, hd), f32),
            vmem((wa, rows, head_cols), f32),
            vmem((pb, ka, rows, 3 * hd), bf16),
            vmem((lanes, hd), bf16),
            vmem((lanes, hd), bf16),
            vmem(kept_shape, f32),
            vmem((1, lanes), f32),
            vmem((1, lanes), f32),
            vmem((1, lanes), f32),
            vmem((1, lanes), f32),
            vmem((rows, 128), f32),
            vmem((members, 1, piece), f32),
            vmem((members, 1, piece), f32),
            sem((5 + wa,)),
            sem((wa,)),
            sem((wa,)),
            sem((wa,)),
            sem((wa,)),
            sem((wa,)),
            sem((wa,)),
            sem((wa,)),
            sem((wa,)),
            sem((pb,)),
            sem((pb,)),
            sem((pb, ka)),
            sem((pb, ka)),
            sem((members,)),
            sem((members,)),
        ],
        compiler_params=pltpu.CompilerParams(
            collective_id=0, has_side_effects=True, vmem_limit_bytes=vmem_limit
        ),
    )(
        clean_rows,
        noised_rows,
        query_weight,
        key_weight,
        value_weight,
        out_grads,
        lookback.reshape(-1, 128),
    )
    return out.reshape(piece)


def solution(mesh):
    in_specs = (
        P(("pairs", "pb", "ka"), "wa"),
        P(("pairs", "pb", "ka"), "wa"),
        P("wa", None),
        P("wa", None),
        P("wa", None),
        P(("pairs", "pb", "ka"), "wa"),
        P("pairs"),
    )
    out_specs = P(("pairs", "pb", "ka", "wa"))
    return jax.shard_map(shards, mesh=mesh, in_specs=in_specs, out_specs=out_specs, check_vma=False)
```

time: 103 us -> 44.5 us (0.43)
  blocking collectives: 57 us -> 0 us
  Pallas kernels: 0 us -> 43.1 us
  matrix products: 17 us -> 0 us
  between operations: 14.2 us -> 0.01 us
  waiting for transfers between devices: 9.68 us -> 0 us
  other arithmetic: 3.36 us -> 0 us
    pallas_call x0 -> x1, Pallas kernels: none -> 43.1 us  [shards(): pl.pallas_call(functools.partial(kernel, sizes), out_shape=jax.ShapeDtype...]
    all_gather x5 -> x0, blocking collectives: 39.2 us -> none  [the longest x1 31.6 us: shards(): key_tile = lax.all_gather(key_side, ('pb', 'wa'), axis=0, tiled=True)]
    unnamed x1 -> x0, blocking collectives: 17.8 us -> none
    dot_general x6 -> x0, matrix products: 17 us -> none  [the longest x1 4.55 us: block_changes(): jnp.einsum('bhd,kd->bhk', query_block, noised_block, preferred_element_ty...]
    reduce_scatter x2 -> x0, waiting for transfers between devices: 9.64 us -> none  [the longest x1 9.64 us: shards(): lax.psum_scatter(jnp.concatenate([jnp.dot(clean_rows, side_weight, prefer...]
    convert_element_type x2 -> x0, other arithmetic: 1.9 us -> none  [the longest x1 0.97 us: shards(): lax.psum_scatter(query_terms, 'wa', scatter_dimension=1, tiled=True)]
  transfers between devices with their start and end apart: 2 -> 0, of which waited for: 1 -> 0; matrix products, arithmetic and copies ran while one was open for 6% -> 0% of each run, Pallas kernels for 0% -> 0%
where the time goes in v1:
time: 44.5 us; the launch traced here: 44.3 us
  Pallas kernels  43.1 us (97%)
  local copies, waits for them, and re-layouts  1.19 us (3%)
    pallas_call x1, Pallas kernels, shards(): pl.pallas_call(functools.partial(kernel, sizes), out_shape=jax.ShapeDtype...  43.1 us
    unnamed x1, local copies, waits for them, and re-layouts  1.19 us

profile of v1, /device:TPU:0, one launch (start us, length us, event | category | flops | bytes accessed | tf_op | source)
XLA Modules:
  0.0 44.3 jit_solution(6473381479462104122)
XLA Ops:
  0.0 43.1 %shard_map.73 = f32[1,128]{1,0:T(1,128)} custom-call(bf16[256,4096]{1,0:T(8,128)(2,1)} %clean_hbm.1, bf16[256,4096]{1,0:T(8,128)(2,1)} %noised_hbm.1, bf16[4096,512]{1,0:T(8,128)(2,1)} %wq_hbm.1, bf16[4096,128]{1,0:T(8,128)(2,1)} %wk_hbm.1, bf16[4096,128]{1,0:T(8,128)(2,1)} %wv_hbm.1, bf16[256,256]{1,0:T(8,128)(2,1)} %grad_hbm.1, s32[16,128]{1,0:T(8,128)} %bitcast.2), custom_call_target="tpu_custom_call" | custom-call | tf_op jit(solution)/shard_map/pallas_call | solution.py:413
  43.1 1.2 %copy.9 = f32[128]{0:T(128)} copy(f32[128]{0:T(128)} %bitcast.3) | data formatting | bytes 1024

commit v2 on v1

--- a/solution.py
+++ b/solution.py
@@ -86,12 +86,22 @@
     def peer(o):
         return lax.rem(x + o, wa)
 
-    loads = [
-        pltpu.make_async_copy(clean_hbm, clean, load_sem.at[0]),
-        pltpu.make_async_copy(wk_hbm, wkv.at[:, pl.ds(0, hd)], load_sem.at[1]),
-        pltpu.make_async_copy(wv_hbm, wkv.at[:, pl.ds(hd, hd)], load_sem.at[2]),
-        pltpu.make_async_copy(noised_hbm, noised, load_sem.at[3]),
-    ]
+    half = clean.shape[1] // 2
+    loads = []
+    for i in range(2):
+        part = pl.ds(i * half, half)
+        loads += [
+            pltpu.make_async_copy(
+                clean_hbm.at[:, part], clean.at[:, part], load_sem.at[5 + wa + 3 * i]
+            ),
+            pltpu.make_async_copy(
+                wk_hbm.at[part], wkv.at[part, pl.ds(0, hd)], load_sem.at[6 + wa + 3 * i]
+            ),
+            pltpu.make_async_copy(
+                wv_hbm.at[part], wkv.at[part, pl.ds(hd, hd)], load_sem.at[7 + wa + 3 * i]
+            ),
+        ]
+    loads.append(pltpu.make_async_copy(noised_hbm, noised, load_sem.at[3]))
     orders = list(range(1, wa)) + [0]
     for o in orders:
         cols = pl.ds(pl.multiple_of(peer(o) * head_cols, 128), head_cols)
@@ -129,7 +139,10 @@
 
     for load in loads[:3]:
         load.wait()
-    kv_part[...] = dot(clean[...], wkv[...])
+    kv_part[...] = dot(clean[:, :half], wkv[:half, :])
+    for load in loads[3:6]:
+        load.wait()
+    kv_part[...] += dot(clean[:, half:], wkv[half:, :])
     pl.semaphore_wait(barrier, members - 1)
     kv_copies = []
     for o in range(1, wa):
@@ -139,7 +152,7 @@
         )
         copy.start()
         kv_copies.append(copy)
-    loads[3].wait()
+    loads[6].wait()
     nk_part[...] = dot(noised[...], wkv[:, :hd])
     nk_copies = []
     for o in range(1, wa):
@@ -151,7 +164,7 @@
         nk_copies.append(copy)
     q_copies = []
     for n, o in enumerate(orders):
-        loads[4 + n].wait()
+        loads[7 + n].wait()
         q_part[o] = dot(clean[...], wq[o])
         if o:
             copy = remote(
@@ -166,46 +179,53 @@
     kv_sum = kv_part[mine, :]
     for o in range(1, wa):
         kv_sum = kv_sum + kv_in[o]
-    side[z, c, mine, pl.ds(0, 2 * hd)] = kv_sum.astype(jnp.bfloat16)
+    side[me, :, pl.ds(0, 2 * hd)] = kv_sum.astype(jnp.bfloat16)
     for copy in nk_copies:
         copy.wait_recv()
     nk_sum = nk_part[mine, :]
     for o in range(1, wa):
         nk_sum = nk_sum + nk_in[o]
-    side[z, c, mine, pl.ds(2 * hd, hd)] = nk_sum.astype(jnp.bfloat16)
-    ag_copies = []
-    for o in range(1, wa):
-        own = side.at[z, c, mine]
-        copy = remote(own, own, ag_send.at[o], ag_recv.at[wa - o], {"wa": peer(o)})
-        copy.start()
-        ag_copies.append(copy)
-    for o in range(1, wa):
-        theirs = side.at[z, c, part_rows(peer(wa - o))]
-        remote(theirs, theirs, ag_send.at[o], ag_recv.at[wa - o], {"wa": peer(o)}).wait_recv()
+    side[me, :, pl.ds(2 * hd, hd)] = nk_sum.astype(jnp.bfloat16)
+
+    def owner(zz, cc, xx):
+        return (zz * ka + cc) * wa + xx
 
     def up(zz):
-        block = side.at[zz, c]
+        block = side.at[owner(zz, c, x)]
         return remote(block, block, z_send.at[zz], z_recv.at[zz], {"pb": z + 1})
 
-    def across(zz, o):
-        block = side.at[zz, c]
+    def along(zz, o):
+        block = side.at[owner(zz, c, x)]
+        return remote(block, block, ag_send.at[zz, o], ag_recv.at[zz, wa - o], {"wa": peer(o)})
+
+    def across(zz, w, o):
+        block = side.at[owner(zz, c, peer(wa - w))]
         return remote(
-            block, block, sib_send.at[zz, o], sib_recv.at[zz, ka - o], {"ka": lax.rem(c + o, ka)}
+            block,
+            block,
+            sib_send.at[zz, w, o],
+            sib_recv.at[zz, w, ka - o],
+            {"ka": lax.rem(c + o, ka)},
         )
+
+    def hand_over(zz, w):
+        for o in range(1, ka):
+
+            @pl.when((zz < z) | (c + o < ka))
+            def _():
+                across(zz, w, o).start()
 
     def pass_on(zz):
         @pl.when(z + 1 < pb)
         def _():
             up(zz).start()
 
-        for o in range(1, ka):
-
-            @pl.when((zz < z) | (c + o < ka))
-            def _():
-                across(zz, o).start()
+        for o in range(1, wa):
+            along(zz, o).start()
+        hand_over(zz, 0)
 
     def arrive(zz):
-        block = side.at[zz, c]
+        block = side.at[owner(zz, c, x)]
         remote(block, block, z_send.at[zz], z_recv.at[zz], {"pb": z - 1}).wait_recv()
         pass_on(zz)
 
@@ -236,12 +256,12 @@
     )
     before_key = last_key - look
 
-    def products(zz, cc):
-        key_pos = (zz * ka + cc) * rows + lax.broadcasted_iota(jnp.int32, (rows, lanes), 0)
+    def products(t):
+        key_pos = t * piece + lax.broadcasted_iota(jnp.int32, (piece, lanes), 0)
         visible = (key_pos <= last_key) & (key_pos > before_key)
-        scores = dot_t(side[zz, cc, :, pl.ds(0, hd)], qs[...]) * scale
-        patched = dot_t(side[zz, cc, :, pl.ds(2 * hd, hd)], qs[...]) * scale
-        grad_value = dot_t(side[zz, cc, :, pl.ds(hd, hd)], gs[...])
+        scores = dot_t(side[t, :, pl.ds(0, hd)], qs[...]) * scale
+        patched = dot_t(side[t, :, pl.ds(2 * hd, hd)], qs[...]) * scale
+        grad_value = dot_t(side[t, :, pl.ds(hd, hd)], gs[...])
         return (
             jnp.where(visible, scores, very_low),
             jnp.where(visible, patched, very_low),
@@ -252,12 +272,12 @@
     total[...] = jnp.zeros((1, lanes), jnp.float32)
     weighted[...] = jnp.zeros((1, lanes), jnp.float32)
 
-    def stats(zz, cc):
-        scores, patched, grad_value = products(zz, cc)
+    def stats(t):
+        scores, patched, grad_value = products(t)
         if keep:
-            kept[zz, cc, 0] = scores
-            kept[zz, cc, 1] = patched
-            kept[zz, cc, 2] = grad_value
+            kept[t, 0] = scores
+            kept[t, 1] = patched
+            kept[t, 2] = grad_value
         highest = jnp.maximum(top[...], jnp.max(scores, axis=0, keepdims=True))
         rescale = jnp.exp2(top[...] - highest)
         weights = jnp.exp2(scores - highest)
@@ -267,52 +287,60 @@
         )
         top[...] = highest
 
-    def other_stats(zz, o):
-        cc = lax.rem(c + ka - o, ka)
-        block = side.at[zz, cc]
-        remote(block, block, sib_send.at[zz, o], sib_recv.at[zz, ka - o], {"ka": cc}).wait_recv()
-        stats(zz, cc)
-
-    stats(z, c)
-    for o in range(1, ka):
-
-        @pl.when(c >= o)
-        def _():
-            other_stats(z, o)
-
-    def earlier(s, carry):
+    def other_cores(zz, w):
+        for o in range(1, ka):
+
+            @pl.when((zz < z) | (c >= o))
+            def _():
+                cc = lax.rem(c + ka - o, ka)
+                t = owner(zz, cc, peer(wa - w))
+                block = side.at[t]
+                remote(
+                    block, block, sib_send.at[zz, w, o], sib_recv.at[zz, w, ka - o], {"ka": cc}
+                ).wait_recv()
+                stats(t)
+
+    def group(s, carry):
         @pl.when(s <= z)
         def _():
-            @pl.when(s >= 2)
+            zz = z - s
+            stats(owner(zz, c, x))
+            other_cores(zz, 0)
+
+            @pl.when((s >= 1) & (s < z))
             def _():
-                arrive(z - s)
-
-            stats(z - s, c)
-            for o in range(1, ka):
-                other_stats(z - s, o)
+                arrive(zz - 1)
+
+            for w in range(1, wa):
+                t = owner(zz, c, peer(wa - w))
+                block = side.at[t]
+                remote(
+                    block, block, ag_send.at[zz, w], ag_recv.at[zz, wa - w], {"wa": peer(w)}
+                ).wait_recv()
+                hand_over(zz, w)
+                stats(t)
+                other_cores(zz, w)
 
         return carry
 
-    lax.fori_loop(1, pb, earlier, 0)
-
-    mean[...] = weighted[...] / jnp.maximum(total[...], 1.0)
-
-    step = 64
+    lax.fori_loop(0, pb, group, 0)
+
+    mean[...] = weighted[...] * pl.reciprocal(jnp.maximum(total[...], 1.0))
+
+    step = 32
 
     def att_copy(t):
         return remote(att.at[t], att_in.at[me], att_send.at[t], att_recv.at[me], place(t))
 
-    def changes(b, carry):
-        zz, cc = b // ka, b % ka
-
-        @pl.when(b <= z * ka + c)
+    def changes(t, carry):
+        @pl.when(t // wa <= z * ka + c)
         def _():
             if not keep:
-                scores, patched, grad_value = products(zz, cc)
-                kept[0, 0, 0] = scores
-                kept[0, 0, 1] = patched
-                kept[0, 0, 2] = grad_value
-            kz, kc = (zz, cc) if keep else (0, 0)
+                scores, patched, grad_value = products(t)
+                kept[0, 0] = scores
+                kept[0, 1] = patched
+                kept[0, 2] = grad_value
+            kt = t if keep else 0
 
             def chunk(k, carry):
                 keys = pl.ds(pl.multiple_of(k * step, step), step)
@@ -320,35 +348,30 @@
                 for q in range(lanes // 128):
                     cols = pl.ds(q * 128, 128)
                     high = top[:, cols]
-                    sums = weighted[:, cols]
-                    away = kept[kz, kc, 1, keys, cols] - high
+                    away = kept[kt, 1, keys, cols] - high
                     small = jnp.exp2(-jnp.abs(away))
                     above = away > 0.0
                     factor = jnp.where(above, small, 1.0)
                     swapped = (
                         jnp.where(above, 1.0, small)
-                        - jnp.exp2(kept[kz, kc, 0, keys, cols] - high) * factor
+                        - jnp.exp2(kept[kt, 0, keys, cols] - high) * factor
                     )
                     divisor = jnp.maximum(total[:, cols] * factor + swapped, 1.0)
-                    so_far = so_far + (
-                        (sums * factor + swapped * kept[kz, kc, 2, keys, cols]) / divisor
-                        - mean[:, cols]
-                    )
+                    upper = weighted[:, cols] * factor + swapped * kept[kt, 2, keys, cols]
+                    so_far = so_far + (upper * pl.reciprocal(divisor) - mean[:, cols])
                 lane_sum[keys, :] = so_far
                 return carry
 
-            lax.fori_loop(0, rows // step, chunk, 0)
-            row = jnp.sum(jnp.transpose(lane_sum[...]), axis=0, keepdims=True)
-            for p in range(wa):
-                att[b * wa + p] = row[:, p * piece : (p + 1) * piece]
-
-                @pl.when(b * wa + p != me)
-                def _():
-                    att_copy(b * wa + p).start()
+            lax.fori_loop(0, piece // step, chunk, 0)
+            att[t] = jnp.sum(jnp.transpose(lane_sum[...]), axis=0, keepdims=True)
+
+            @pl.when(t != me)
+            def _():
+                att_copy(t).start()
 
         return carry
 
-    lax.fori_loop(0, pb * ka, changes, 0)
+    lax.fori_loop(0, members, changes, 0)
 
     out_ref[...] = att[me]
 
@@ -364,7 +387,7 @@
 
     lax.fori_loop(0, members, collect, 0)
 
-    for copy in kv_copies + nk_copies + q_copies + ag_copies:
+    for copy in kv_copies + nk_copies + q_copies:
         copy.wait_send()
 
     def drain(zz, carry):
@@ -374,11 +397,14 @@
             def _():
                 up(zz).wait_send()
 
-            for o in range(1, ka):
-
-                @pl.when((zz < z) | (c + o < ka))
-                def _():
-                    across(zz, o).wait_send()
+            for o in range(1, wa):
+                along(zz, o).wait_send()
+            for w in range(wa):
+                for o in range(1, ka):
+
+                    @pl.when((zz < z) | (c + o < ka))
+                    def _():
+                        across(zz, w, o).wait_send()
 
         return carry
 
@@ -403,9 +429,8 @@
     lanes = heads * rows
     piece = rows // wa
     members = pb * ka * wa
-    block = 3 * rows * lanes * 4
-    keep = pb * ka * block <= keep_limit
-    kept_shape = (pb, ka, 3, rows, lanes) if keep else (1, 1, 3, rows, lanes)
+    keep = members * 3 * piece * lanes * 4 <= keep_limit
+    kept_shape = (members if keep else 1, 3, piece, lanes)
     sizes = (pb, ka, wa, rows, hd, heads, keep)
     bf16, f32 = jnp.bfloat16, jnp.float32
     vmem = pltpu.VMEM
@@ -427,7 +452,7 @@
             vmem((wa, piece, 2 * hd), f32),
             vmem((wa, piece, hd), f32),
             vmem((wa, rows, head_cols), f32),
-            vmem((pb, ka, rows, 3 * hd), bf16),
+            vmem((members, piece, 3 * hd), bf16),
             vmem((lanes, hd), bf16),
             vmem((lanes, hd), bf16),
             vmem(kept_shape, f32),
@@ -435,22 +460,22 @@
             vmem((1, lanes), f32),
             vmem((1, lanes), f32),
             vmem((1, lanes), f32),
-            vmem((rows, 128), f32),
+            vmem((piece, 128), f32),
             vmem((members, 1, piece), f32),
             vmem((members, 1, piece), f32),
-            sem((5 + wa,)),
+            sem((11 + wa,)),
             sem((wa,)),
             sem((wa,)),
             sem((wa,)),
             sem((wa,)),
             sem((wa,)),
             sem((wa,)),
-            sem((wa,)),
-            sem((wa,)),
+            sem((pb, wa)),
+            sem((pb, wa)),
             sem((pb,)),
             sem((pb,)),
-            sem((pb, ka)),
-            sem((pb, ka)),
+            sem((pb, wa, ka)),
+            sem((pb, wa, ka)),
             sem((members,)),
             sem((members,)),
         ],

time: 44.5 us -> 39.2 us (0.88); the launches traced: 44.3 us -> 38.6 us
  Pallas kernels: 43.1 us -> 37.4 us
    pallas_call x1, Pallas kernels: 43.1 us -> 37.4 us  [shards(): pl.pallas_call(functools.partial(kernel, sizes), out_shape=jax.ShapeDtype...]
where the time goes in v2:
time: 39.2 us; the launch traced here: 38.6 us
  Pallas kernels  37.4 us (95%)
  local copies, waits for them, and re-layouts  1.19 us (3%)
    pallas_call x1, Pallas kernels, shards(): pl.pallas_call(functools.partial(kernel, sizes), out_shape=jax.ShapeDtype...  37.4 us
    unnamed x1, local copies, waits for them, and re-layouts  1.19 us

profile of v2, /device:TPU:0, one launch (start us, length us, event | category | flops | bytes accessed | tf_op | source)
XLA Modules:
  0.0 38.6 jit_solution(13802638363204981510)
XLA Ops:
  0.0 37.4 %shard_map.73 = f32[1,128]{1,0:T(1,128)} custom-call(bf16[256,4096]{1,0:T(8,128)(2,1)} %clean_hbm.1, bf16[256,4096]{1,0:T(8,128)(2,1)} %noised_hbm.1, bf16[4096,512]{1,0:T(8,128)(2,1)} %wq_hbm.1, bf16[4096,128]{1,0:T(8,128)(2,1)} %wk_hbm.1, bf16[4096,128]{1,0:T(8,128)(2,1)} %wv_hbm.1, bf16[256,256]{1,0:T(8,128)(2,1)} %grad_hbm.1, s32[16,128]{1,0:T(8,128)} %bitcast.2), custom_call_target="tpu_custom_call" | custom-call | tf_op jit(solution)/shard_map/pallas_call | solution.py:438
  37.4 1.2 %copy.9 = f32[128]{0:T(128)} copy(f32[128]{0:T(128)} %bitcast.3) | data formatting | bytes 1024

commit v3 on v2

--- a/solution.py
+++ b/solution.py
@@ -11,6 +11,7 @@
 very_low = -1e30
 keep_limit = 24 * 2**20
 vmem_limit = 56 * 2**20
+reach = 2
 MESH = pl.DeviceIdType.MESH
 
 
@@ -32,7 +33,7 @@
     wk_hbm,
     wv_hbm,
     grad_hbm,
-    look_ref,
+    look_hbm,
     out_ref,
     clean,
     noised,
@@ -56,6 +57,7 @@
     lane_sum,
     att,
     att_in,
+    look_ref,
     load_sem,
     kv_send,
     kv_recv,
@@ -67,6 +69,8 @@
     ag_recv,
     z_send,
     z_recv,
+    next_send,
+    next_recv,
     sib_send,
     sib_recv,
     att_send,
@@ -107,6 +111,7 @@
         cols = pl.ds(pl.multiple_of(peer(o) * head_cols, 128), head_cols)
         loads.append(pltpu.make_async_copy(wq_hbm.at[:, cols], wq.at[o], load_sem.at[5 + o]))
     loads.append(pltpu.make_async_copy(grad_hbm, grad, load_sem.at[4]))
+    loads.append(pltpu.make_async_copy(look_hbm, look_ref, load_sem.at[0]))
     for load in loads:
         load.start()
 
@@ -208,6 +213,16 @@
             {"ka": lax.rem(c + o, ka)},
         )
 
+    def next_up(zz, w):
+        block = side.at[owner(zz, c, peer(wa - w))]
+        return remote(block, block, next_send.at[zz, w], next_recv.at[zz, w], {"pb": z + 1})
+
+    def goes_up(zz):
+        return (z + 1 < pb) & (z + 1 - zz <= reach)
+
+    def goes_along(zz):
+        return (zz == z) | (z - zz > reach)
+
     def hand_over(zz, w):
         for o in range(1, ka):
 
@@ -220,9 +235,33 @@
         def _():
             up(zz).start()
 
-        for o in range(1, wa):
-            along(zz, o).start()
+        @pl.when(goes_along(zz))
+        def _():
+            for o in range(1, wa):
+                along(zz, o).start()
+
         hand_over(zz, 0)
+
+    def exchanged(zz, w):
+        block = side.at[owner(zz, c, peer(wa - w))]
+
+        @pl.when(goes_along(zz))
+        def _():
+            remote(
+                block, block, ag_send.at[zz, w], ag_recv.at[zz, wa - w], {"wa": peer(w)}
+            ).wait_recv()
+
+        @pl.when(~goes_along(zz))
+        def _():
+            remote(
+                block, block, next_send.at[zz, w], next_recv.at[zz, w], {"pb": z - 1}
+            ).wait_recv()
+
+        @pl.when(goes_up(zz))
+        def _():
+            next_up(zz, w).start()
+
+        hand_over(zz, w)
 
     def arrive(zz):
         block = side.at[owner(zz, c, x)]
@@ -235,6 +274,10 @@
     def _():
         arrive(z - 1)
 
+    for w in range(1, wa):
+        exchanged(z, w)
+
+    loads[-2].wait()
     loads[-1].wait()
     for copy in q_copies:
         copy.wait_recv()
@@ -312,13 +355,12 @@
                 arrive(zz - 1)
 
             for w in range(1, wa):
-                t = owner(zz, c, peer(wa - w))
-                block = side.at[t]
-                remote(
-                    block, block, ag_send.at[zz, w], ag_recv.at[zz, wa - w], {"wa": peer(w)}
-                ).wait_recv()
-                hand_over(zz, w)
-                stats(t)
+
+                @pl.when(s >= 1)
+                def _():
+                    exchanged(zz, w)
+
+                stats(owner(zz, c, peer(wa - w)))
                 other_cores(zz, w)
 
         return carry
@@ -397,8 +439,16 @@
             def _():
                 up(zz).wait_send()
 
-            for o in range(1, wa):
-                along(zz, o).wait_send()
+            @pl.when(goes_along(zz))
+            def _():
+                for o in range(1, wa):
+                    along(zz, o).wait_send()
+
+            @pl.when(goes_up(zz))
+            def _():
+                for w in range(1, wa):
+                    next_up(zz, w).wait_send()
+
             for w in range(wa):
                 for o in range(1, ka):
 
@@ -438,7 +488,7 @@
     out = pl.pallas_call(
         functools.partial(kernel, sizes),
         out_shape=jax.ShapeDtypeStruct((1, piece), f32),
-        in_specs=[pl.BlockSpec(memory_space=pl.ANY)] * 6 + [pl.BlockSpec(memory_space=vmem)],
+        in_specs=[pl.BlockSpec(memory_space=pl.ANY)] * 7,
         out_specs=pl.BlockSpec(memory_space=vmem),
         scratch_shapes=[
             vmem((rows, depth), bf16),
@@ -463,6 +513,7 @@
             vmem((piece, 128), f32),
             vmem((members, 1, piece), f32),
             vmem((members, 1, piece), f32),
+            vmem((members * piece // 128, 128), jnp.int32),
             sem((11 + wa,)),
             sem((wa,)),
             sem((wa,)),
@@ -474,6 +525,8 @@
             sem((pb, wa)),
             sem((pb,)),
             sem((pb,)),
+            sem((pb, wa)),
+            sem((pb, wa)),
             sem((pb, wa, ka)),
             sem((pb, wa, ka)),
             sem((members,)),

time: 39.2 us -> 38.5 us (0.982)
  Pallas kernels: 37.4 us -> 36.9 us
    pallas_call x1, Pallas kernels: 37.4 us -> 36.9 us  [shards(): pl.pallas_call(functools.partial(kernel, sizes), out_shape=jax.ShapeDtype...]
where the time goes in v3:
time: 38.5 us; the launch traced here: 38.1 us
  Pallas kernels  36.9 us (96%)
  local copies, waits for them, and re-layouts  1.19 us (3%)
    pallas_call x1, Pallas kernels, shards(): pl.pallas_call(functools.partial(kernel, sizes), out_shape=jax.ShapeDtype...  36.9 us
    unnamed x1, local copies, waits for them, and re-layouts  1.19 us

profile of v3, /device:TPU:0, one launch (start us, length us, event | category | flops | bytes accessed | tf_op | source)
XLA Modules:
  0.0 38.1 jit_solution(6680348843229790739)
XLA Ops:
  0.0 36.9 %shard_map.73 = f32[1,128]{1,0:T(1,128)} custom-call(bf16[256,4096]{1,0:T(8,128)(2,1)} %clean_hbm.1, bf16[256,4096]{1,0:T(8,128)(2,1)} %noised_hbm.1, bf16[4096,512]{1,0:T(8,128)(2,1)} %wq_hbm.1, bf16[4096,128]{1,0:T(8,128)(2,1)} %wk_hbm.1, bf16[4096,128]{1,0:T(8,128)(2,1)} %wv_hbm.1, bf16[256,256]{1,0:T(8,128)(2,1)} %grad_hbm.1, s32[16,128]{1,0:T(8,128)} %bitcast.2), custom_call_target="tpu_custom_call" | custom-call | tf_op jit(solution)/shard_map/pallas_call | solution.py:488
  36.9 1.2 %copy.9 = f32[128]{0:T(128)} copy(f32[128]{0:T(128)} %bitcast.3) | data formatting | bytes 1024

commit v4 on v3

--- a/solution.py
+++ b/solution.py
@@ -17,12 +17,6 @@
 
 def dot(left, right):
     return jnp.dot(left, right, preferred_element_type=jnp.float32)
-
-
-def dot_t(left, right):
-    return lax.dot_general(
-        left, right, (((1,), (1,)), ((), ())), preferred_element_type=jnp.float32
-    )
 
 
 def kernel(
@@ -168,15 +162,14 @@
         copy.start()
         nk_copies.append(copy)
     q_copies = []
-    for n, o in enumerate(orders):
+    for n, o in enumerate(orders[:-1]):
         loads[7 + n].wait()
         q_part[o] = dot(clean[...], wq[o])
-        if o:
-            copy = remote(
-                q_part.at[o], q_in.at[wa - o], q_send.at[o], q_recv.at[wa - o], {"wa": peer(o)}
-            )
-            copy.start()
-            q_copies.append(copy)
+        copy = remote(
+            q_part.at[o], q_in.at[wa - o], q_send.at[o], q_recv.at[wa - o], {"wa": peer(o)}
+        )
+        copy.start()
+        q_copies.append(copy)
 
     mine = part_rows(x)
     for copy in kv_copies:
@@ -269,6 +262,8 @@
         pass_on(zz)
 
     pass_on(z)
+    loads[6 + wa].wait()
+    q_part[0] = dot(clean[...], wq[0])
 
     @pl.when(z >= 1)
     def _():
@@ -286,8 +281,8 @@
         q_sum = q_sum + q_in[o]
     q_sum = q_sum.astype(jnp.bfloat16)
     for h in range(heads):
-        qs[pl.ds(h * rows, rows), :] = q_sum[:, h * hd : (h + 1) * hd]
-        gs[pl.ds(h * rows, rows), :] = grad[:, h * hd : (h + 1) * hd]
+        qs[:, pl.ds(h * rows, rows)] = jnp.transpose(q_sum[:, h * hd : (h + 1) * hd])
+        gs[:, pl.ds(h * rows, rows)] = jnp.transpose(grad[:, h * hd : (h + 1) * hd])
 
     group_rows = rows // 128
     first_look = (z * ka + c) * group_rows
@@ -302,9 +297,13 @@
     def products(t):
         key_pos = t * piece + lax.broadcasted_iota(jnp.int32, (piece, lanes), 0)
         visible = (key_pos <= last_key) & (key_pos > before_key)
-        scores = dot_t(side[t, :, pl.ds(0, hd)], qs[...]) * scale
-        patched = dot_t(side[t, :, pl.ds(2 * hd, hd)], qs[...]) * scale
-        grad_value = dot_t(side[t, :, pl.ds(hd, hd)], gs[...])
+        both = dot(
+            jnp.concatenate([side[t, :, pl.ds(0, hd)], side[t, :, pl.ds(2 * hd, hd)]], axis=0),
+            qs[...],
+        )
+        scores = both[:piece] * scale
+        patched = both[piece:] * scale
+        grad_value = dot(side[t, :, pl.ds(hd, hd)], gs[...])
         return (
             jnp.where(visible, scores, very_low),
             jnp.where(visible, patched, very_low),
@@ -367,7 +366,9 @@
 
     lax.fori_loop(0, pb, group, 0)
 
-    mean[...] = weighted[...] * pl.reciprocal(jnp.maximum(total[...], 1.0))
+    mean[...] = weighted[...] * pl.reciprocal(
+        jnp.maximum(total[...], 1.0), full_range=False
+    )
 
     step = 32
 
@@ -400,7 +401,7 @@
                     )
                     divisor = jnp.maximum(total[:, cols] * factor + swapped, 1.0)
                     upper = weighted[:, cols] * factor + swapped * kept[kt, 2, keys, cols]
-                    so_far = so_far + (upper * pl.reciprocal(divisor) - mean[:, cols])
+                    so_far = so_far + (upper * pl.reciprocal(divisor, full_range=False) - mean[:, cols])
                 lane_sum[keys, :] = so_far
                 return carry
 
@@ -503,8 +504,8 @@
             vmem((wa, piece, hd), f32),
             vmem((wa, rows, head_cols), f32),
             vmem((members, piece, 3 * hd), bf16),
-            vmem((lanes, hd), bf16),
-            vmem((lanes, hd), bf16),
+            vmem((hd, lanes), bf16),
+            vmem((hd, lanes), bf16),
             vmem(kept_shape, f32),
             vmem((1, lanes), f32),
             vmem((1, lanes), f32),

time: 38.5 us -> 38.5 us (level)
  no operation moved by 1% of the time
where the time goes in v4:
time: 38.5 us; the launch traced here: 38 us
  Pallas kernels  36.8 us (96%)
  local copies, waits for them, and re-layouts  1.19 us (3%)
    pallas_call x1, Pallas kernels, shards(): pl.pallas_call(functools.partial(kernel, sizes), out_shape=jax.ShapeDtype...  36.8 us
    unnamed x1, local copies, waits for them, and re-layouts  1.19 us

profile of v4, /device:TPU:0, one launch (start us, length us, event | category | flops | bytes accessed | tf_op | source)
XLA Modules:
  0.0 38.0 jit_solution(8948173651435903581)
XLA Ops:
  0.0 36.8 %shard_map.73 = f32[1,128]{1,0:T(1,128)} custom-call(bf16[256,4096]{1,0:T(8,128)(2,1)} %clean_hbm.1, bf16[256,4096]{1,0:T(8,128)(2,1)} %noised_hbm.1, bf16[4096,512]{1,0:T(8,128)(2,1)} %wq_hbm.1, bf16[4096,128]{1,0:T(8,128)(2,1)} %wk_hbm.1, bf16[4096,128]{1,0:T(8,128)(2,1)} %wv_hbm.1, bf16[256,256]{1,0:T(8,128)(2,1)} %grad_hbm.1, s32[16,128]{1,0:T(8,128)} %bitcast.2), custom_call_target="tpu_custom_call" | custom-call | tf_op jit(solution)/shard_map/pallas_call | solution.py:489
  36.8 1.2 %copy.9 = f32[128]{0:T(128)} copy(f32[128]{0:T(128)} %bitcast.3) | data formatting | bytes 1024

commit v5 on v4

--- a/solution.py
+++ b/solution.py
@@ -48,7 +48,6 @@
     total,
     weighted,
     mean,
-    lane_sum,
     att,
     att_in,
     look_ref,
@@ -314,57 +313,65 @@
     total[...] = jnp.zeros((1, lanes), jnp.float32)
     weighted[...] = jnp.zeros((1, lanes), jnp.float32)
 
-    def stats(t):
-        scores, patched, grad_value = products(t)
-        if keep:
-            kept[t, 0] = scores
-            kept[t, 1] = patched
-            kept[t, 2] = grad_value
-        highest = jnp.maximum(top[...], jnp.max(scores, axis=0, keepdims=True))
+    def stats(pieces):
+        parts = []
+        highest = top[...]
+        for t in pieces:
+            scores, patched, grad_value = products(t)
+            if keep:
+                kept[t, 0] = scores
+                kept[t, 1] = patched
+                kept[t, 2] = grad_value
+            parts.append((scores, grad_value))
+            highest = jnp.maximum(highest, jnp.max(scores, axis=0, keepdims=True))
         rescale = jnp.exp2(top[...] - highest)
-        weights = jnp.exp2(scores - highest)
-        total[...] = total[...] * rescale + jnp.sum(weights, axis=0, keepdims=True)
-        weighted[...] = weighted[...] * rescale + jnp.sum(
-            weights * grad_value, axis=0, keepdims=True
-        )
+        sums = total[...] * rescale
+        products_sum = weighted[...] * rescale
+        for scores, grad_value in parts:
+            weights = jnp.exp2(scores - highest)
+            sums = sums + jnp.sum(weights, axis=0, keepdims=True)
+            products_sum = products_sum + jnp.sum(weights * grad_value, axis=0, keepdims=True)
+        total[...] = sums
+        weighted[...] = products_sum
         top[...] = highest
 
-    def other_cores(zz, w):
-        for o in range(1, ka):
-
-            @pl.when((zz < z) | (c >= o))
-            def _():
-                cc = lax.rem(c + ka - o, ka)
-                t = owner(zz, cc, peer(wa - w))
-                block = side.at[t]
-                remote(
-                    block, block, sib_send.at[zz, w, o], sib_recv.at[zz, w, ka - o], {"ka": cc}
-                ).wait_recv()
-                stats(t)
+    def lanes_of(zz, cc):
+        return [owner(zz, cc, xx) for xx in range(wa)]
+
+    def other_core(zz, o):
+        cc = lax.rem(c + ka - o, ka)
+        for w in range(wa):
+            block = side.at[owner(zz, cc, peer(wa - w))]
+            remote(
+                block, block, sib_send.at[zz, w, o], sib_recv.at[zz, w, ka - o], {"ka": cc}
+            ).wait_recv()
+
+    stats(lanes_of(z, c))
+    for o in range(1, ka):
+
+        @pl.when(c >= o)
+        def _():
+            other_core(z, o)
+            stats(lanes_of(z, lax.rem(c + ka - o, ka)))
 
     def group(s, carry):
         @pl.when(s <= z)
         def _():
             zz = z - s
-            stats(owner(zz, c, x))
-            other_cores(zz, 0)
-
-            @pl.when((s >= 1) & (s < z))
+
+            @pl.when(s < z)
             def _():
                 arrive(zz - 1)
 
             for w in range(1, wa):
-
-                @pl.when(s >= 1)
-                def _():
-                    exchanged(zz, w)
-
-                stats(owner(zz, c, peer(wa - w)))
-                other_cores(zz, w)
+                exchanged(zz, w)
+            for o in range(1, ka):
+                other_core(zz, o)
+            stats([t for cc in range(ka) for t in lanes_of(zz, cc)])
 
         return carry
 
-    lax.fori_loop(0, pb, group, 0)
+    lax.fori_loop(1, pb, group, 0)
 
     mean[...] = weighted[...] * pl.reciprocal(
         jnp.maximum(total[...], 1.0), full_range=False
@@ -375,46 +382,51 @@
     def att_copy(t):
         return remote(att.at[t], att_in.at[me], att_send.at[t], att_recv.at[me], place(t))
 
-    def changes(t, carry):
-        @pl.when(t // wa <= z * ka + c)
-        def _():
-            if not keep:
-                scores, patched, grad_value = products(t)
-                kept[0, 0] = scores
-                kept[0, 1] = patched
-                kept[0, 2] = grad_value
-            kt = t if keep else 0
-
-            def chunk(k, carry):
-                keys = pl.ds(pl.multiple_of(k * step, step), step)
-                so_far = jnp.zeros((step, 128), jnp.float32)
-                for q in range(lanes // 128):
-                    cols = pl.ds(q * 128, 128)
-                    high = top[:, cols]
-                    away = kept[kt, 1, keys, cols] - high
-                    small = jnp.exp2(-jnp.abs(away))
-                    above = away > 0.0
-                    factor = jnp.where(above, small, 1.0)
-                    swapped = (
-                        jnp.where(above, 1.0, small)
-                        - jnp.exp2(kept[kt, 0, keys, cols] - high) * factor
-                    )
-                    divisor = jnp.maximum(total[:, cols] * factor + swapped, 1.0)
-                    upper = weighted[:, cols] * factor + swapped * kept[kt, 2, keys, cols]
-                    so_far = so_far + (upper * pl.reciprocal(divisor, full_range=False) - mean[:, cols])
-                lane_sum[keys, :] = so_far
-                return carry
-
-            lax.fori_loop(0, piece // step, chunk, 0)
-            att[t] = jnp.sum(jnp.transpose(lane_sum[...]), axis=0, keepdims=True)
-
-            @pl.when(t != me)
-            def _():
-                att_copy(t).start()
+    def piece_changes(t, slot):
+        kt = t if keep else slot
+        if not keep:
+            scores, patched, grad_value = products(t)
+            kept[kt, 0] = scores
+            kept[kt, 1] = patched
+            kept[kt, 2] = grad_value
+        columns = []
+        for k in range(piece // step):
+            keys = pl.ds(k * step, step)
+            so_far = jnp.zeros((step, 128), jnp.float32)
+            for q in range(lanes // 128):
+                cols = pl.ds(q * 128, 128)
+                high = top[:, cols]
+                away = kept[kt, 1, keys, cols] - high
+                small = jnp.exp2(-jnp.abs(away))
+                above = away > 0.0
+                factor = jnp.where(above, small, 1.0)
+                swapped = (
+                    jnp.where(above, 1.0, small)
+                    - jnp.exp2(kept[kt, 0, keys, cols] - high) * factor
+                )
+                divisor = jnp.maximum(total[:, cols] * factor + swapped, 1.0)
+                upper = weighted[:, cols] * factor + swapped * kept[kt, 2, keys, cols]
+                inverse = pl.reciprocal(divisor, full_range=False)
+                so_far = so_far + (upper * inverse - mean[:, cols])
+            columns.append(so_far)
+        summed = jnp.concatenate(columns, axis=0)
+        return jnp.sum(jnp.transpose(summed), axis=0, keepdims=True)
+
+    def changes(b, carry):
+        @pl.when(b <= z * ka + c)
+        def _():
+            result = [piece_changes(b * wa + p, p) for p in range(wa)]
+            for p in range(wa):
+                att[b * wa + p] = result[p]
+            for p in range(wa):
+
+                @pl.when(b * wa + p != me)
+                def _():
+                    att_copy(b * wa + p).start()
 
         return carry
 
-    lax.fori_loop(0, members, changes, 0)
+    lax.fori_loop(0, pb * ka, changes, 0)
 
     out_ref[...] = att[me]
 
@@ -481,7 +493,7 @@
     piece = rows // wa
     members = pb * ka * wa
     keep = members * 3 * piece * lanes * 4 <= keep_limit
-    kept_shape = (members if keep else 1, 3, piece, lanes)
+    kept_shape = (members if keep else wa, 3, piece, lanes)
     sizes = (pb, ka, wa, rows, hd, heads, keep)
     bf16, f32 = jnp.bfloat16, jnp.float32
     vmem = pltpu.VMEM
@@ -511,7 +523,6 @@
             vmem((1, lanes), f32),
             vmem((1, lanes), f32),
             vmem((1, lanes), f32),
-            vmem((piece, 128), f32),
             vmem((members, 1, piece), f32),
             vmem((members, 1, piece), f32),
             vmem((members * piece // 128, 128), jnp.int32),

time: 38.5 us -> 38.5 us (level)
  no operation moved by 1% of the time
where the time goes in v5:
time: 38.5 us; the launch traced here: 38.3 us
  Pallas kernels  37.1 us (96%)
  local copies, waits for them, and re-layouts  1.19 us (3%)
    pallas_call x1, Pallas kernels, shards(): pl.pallas_call(functools.partial(kernel, sizes), out_shape=jax.ShapeDtype...  37.1 us
    unnamed x1, local copies, waits for them, and re-layouts  1.19 us

profile of v5, /device:TPU:0, one launch (start us, length us, event | category | flops | bytes accessed | tf_op | source)
XLA Modules:
  0.0 38.3 jit_solution(5233700486636645924)
XLA Ops:
  0.0 37.1 %shard_map.73 = f32[1,128]{1,0:T(1,128)} custom-call(bf16[256,4096]{1,0:T(8,128)(2,1)} %clean_hbm.1, bf16[256,4096]{1,0:T(8,128)(2,1)} %noised_hbm.1, bf16[4096,512]{1,0:T(8,128)(2,1)} %wq_hbm.1, bf16[4096,128]{1,0:T(8,128)(2,1)} %wk_hbm.1, bf16[4096,128]{1,0:T(8,128)(2,1)} %wv_hbm.1, bf16[256,256]{1,0:T(8,128)(2,1)} %grad_hbm.1, s32[16,128]{1,0:T(8,128)} %bitcast.2), custom_call_target="tpu_custom_call" | custom-call | tf_op jit(solution)/shard_map/pallas_call | solution.py:501
  37.2 1.2 %copy.9 = f32[128]{0:T(128)} copy(f32[128]{0:T(128)} %bitcast.3) | data formatting | bytes 1024

commit v6 on v5

--- a/solution.py
+++ b/solution.py
@@ -268,6 +268,10 @@
     def _():
         arrive(z - 1)
 
+    @pl.when(z >= 2)
+    def _():
+        arrive(z - 2)
+
     for w in range(1, wa):
         exchanged(z, w)
 
@@ -359,9 +363,9 @@
         def _():
             zz = z - s
 
-            @pl.when(s < z)
+            @pl.when(zz >= 2)
             def _():
-                arrive(zz - 1)
+                arrive(zz - 2)
 
             for w in range(1, wa):
                 exchanged(zz, w)

time: 38.5 us -> 38.3 us (level)
  no operation moved by 1% of the time
where the time goes in v6:
time: 38.3 us; the launch traced here: 38.1 us
  Pallas kernels  36.9 us (96%)
  local copies, waits for them, and re-layouts  1.19 us (3%)
    pallas_call x1, Pallas kernels, shards(): pl.pallas_call(functools.partial(kernel, sizes), out_shape=jax.ShapeDtype...  36.9 us
    unnamed x1, local copies, waits for them, and re-layouts  1.19 us

profile of v6, /device:TPU:0, one launch (start us, length us, event | category | flops | bytes accessed | tf_op | source)
XLA Modules:
  0.0 38.1 jit_solution(10044100116247265659)
XLA Ops:
  0.0 36.9 %shard_map.73 = f32[1,128]{1,0:T(1,128)} custom-call(bf16[256,4096]{1,0:T(8,128)(2,1)} %clean_hbm.1, bf16[256,4096]{1,0:T(8,128)(2,1)} %noised_hbm.1, bf16[4096,512]{1,0:T(8,128)(2,1)} %wq_hbm.1, bf16[4096,128]{1,0:T(8,128)(2,1)} %wk_hbm.1, bf16[4096,128]{1,0:T(8,128)(2,1)} %wv_hbm.1, bf16[256,256]{1,0:T(8,128)(2,1)} %grad_hbm.1, s32[16,128]{1,0:T(8,128)} %bitcast.2), custom_call_target="tpu_custom_call" | custom-call | tf_op jit(solution)/shard_map/pallas_call | solution.py:505
  36.9 1.2 %copy.9 = f32[128]{0:T(128)} copy(f32[128]{0:T(128)} %bitcast.3) | data formatting | bytes 1024
